TPU v7x, 32 devices: a whole 2x2x4 slice. The times are simulated.
32 devices in a mesh: dp: 8 (over y, x, core), tensor: 4 (over z).
Axes of the slice: x: 2, y: 2, z: 4, core: 2. Of those that a mesh axis runs over, the one named last changes fastest.
Arguments:
- tokens: bfloat16 [8192, 1024], P(('dp', 'tensor')), may hold values from -6 to 6
- document_lengths: int32 [512], replicated, may hold values from 1 to 512, 8192 in all
- query_proj_weight: bfloat16 [1024, 1024], P(None, 'tensor'), may hold values from -0.1875 to 0.1875
- query_proj_bias: bfloat16 [1024], P('tensor'), may hold values from -3 to 3
- key_proj_weight: bfloat16 [1024, 1024], P(None, 'tensor'), may hold values from -0.1875 to 0.1875
- value_proj_weight: bfloat16 [1024, 1024], P(None, 'tensor'), may hold values from -0.1875 to 0.1875
- value_proj_bias: bfloat16 [1024], P('tensor'), may hold values from -3 to 3
- query_adapter_down: bfloat16 [1024, 8], replicated, may hold values from -0.1875 to 0.1875
- value_adapter_down: bfloat16 [1024, 8], replicated, may hold values from -0.1875 to 0.1875
- query_adapter_up: bfloat16 [8, 1024], P(None, 'tensor'), may hold values from -1 to 1
- value_adapter_up: bfloat16 [8, 1024], P(None, 'tensor'), may hold values from -1 to 1
- attention_out_weight: bfloat16 [1024, 1024], P('tensor'), may hold values from -0.75 to 0.75
- attention_out_bias: bfloat16 [1024], replicated, may hold values from -3 to 3
- attention_norm_gain: bfloat16 [1024], replicated, may hold values from 0.25 to 1.75
- attention_norm_bias: bfloat16 [1024], replicated, may hold values from -3 to 3
- up_proj_weight: bfloat16 [1024, 4096], P(None, 'tensor'), may hold values from -0.1875 to 0.1875
- up_proj_bias: bfloat16 [4096], P('tensor'), may hold values from -3 to 3
- down_proj_weight: bfloat16 [4096, 1024], P('tensor'), may hold values from -0.125 to 0.125
- down_proj_bias: bfloat16 [1024], replicated, may hold values from -3 to 3
- feedforward_norm_gain: bfloat16 [1024], replicated, may hold values from 0.25 to 1.75
- feedforward_norm_bias: bfloat16 [1024], replicated, may hold values from -3 to 3
- cotangent: bfloat16 [8192, 1024], P(('dp', 'tensor')), may hold values from -6 to 6
Outputs:
- output: bfloat16 [8192, 1024], P(('dp', 'tensor'))
- grad_tokens: bfloat16 [8192, 1024], P(('dp', 'tensor'))
- grad_lora_b_query: float32 [8, 1024], P(None, 'tensor')
- grad_lora_b_value: float32 [8, 1024], P(None, 'tensor')
Inputs may be any that keep to these rules, and one draw needn't show every extreme that they name: `document_lengths`: the documents lie one after another over the 8192 positions of the stream and fill it; at least one document has exactly 512 tokens, none has more.
All inputs are finite; a program needn't handle non-finite values.
Results may differ from a plain program's by a relative error of at most 0.017.
The roundings to bfloat16 on the way count: a program that leaves them out, or rounds other values in their place, can miss the bound.
Values may be sent and summed in bfloat16 or wider, within the bound.
A program may use at most 128 MiB of HBM per device.

v0:
```python
import math

import jax
import jax.numpy as jnp
from jax import lax
from jax.experimental import pallas as pl
from jax.experimental.pallas import tpu as pltpu
from jax.sharding import PartitionSpec as P

MESH = pl.DeviceIdType.MESH
HD = 64
MAXLEN = 512
GROUP = 8
LANES = 128
NORM_EPS = 1e-05
MASKED = -1e30
STEPS = {
    "S": "first", "n": "neighbours", "c": "chain1", "C": "chain2", "x": "ends", "y": "chain3", "t": "third", "l": "last",
}
PLAN_BACK = (
    "S2", "S0", "n2", "c0", "S1", "Q2", "c2", "c1", "n0", "S3", "C0", "Q6", "n1", "x2", "c3", "y0", "C2", "Q0",
    "C1", "x0", "n3", "x1", "t2", "y2", "Kn24", "C3", "Q4", "y1", "t0", "x3", "l0", "Kn20", "t3", "t1", "l1", "l2",
    "y3", "Kst0", "Kst4", "l3", "V", "G", "L", "H", "I", "J",
)
PLAN = (
    "+q1", "+q0", "S2", "0q11", "0q01", "1q11", "0q12", "0q02", "2q11", "1q01", "S3", "0q03", "+o", "+u0", "c3",
    "2q01", "1q02", "1q03", "0o1", "0o2", "0q13", "+u1", "0u01", "1q13", "+d1", "0u11", "S1", "2q13", "S0", "1u01",
    "P20", "1q12", "2q03", "0u02", "0u12", "3q11", "n2", "2q02", "n3", "c1", "C3", "3q01", "3q13", "2q12", "1u02",
    "1u11", "3q02", "2u01", "3q12", "3q03", "n1", "c2", "1o1", "n0", "x3", "+d0", "P2", "c0", "1o2", "x2", "1u12",
    "C1", "2u11", "Pn", "x1", "x0", "t2", "2o1", "2o2", "0o3", "t0", "0d11", "A002", "t1", "0u03", "3u01", "1o3",
    "0d01", "2u12", "3o1", "C2", "t3", "2u02", "3o2", "Pt", "0d02", "3u11", "y3", "2o3", "A402", "C0", "0d12",
    "0u13", "l3", "3o3", "y0", "y2", "y1", "Ps", "1u03", "l0", "1d11", "A024", "A424", "l2", "1d01", "1u13", "l1",
    "2u03", "1d02", "0d13", "2d11", "Pl", "A445", "1d12", "2d01", "0d03", "2d02", "2u13", "A045", "3u12", "M", "U1",
    "3u02", "1d13", "2d12", "3u13", "U0", "3d01", "1d03", "3d11", "D1", "3d12", "2d13", "U2", "3d02", "3u03",
    "2d03", "U3", "D2", "D0", "3d03", "3d13", "D3",
)
F32 = jnp.float32
BF16 = jnp.bfloat16


def dot(left, right):
    return lax.dot_general(left, right, (((1,), (0,)), ((), ())), preferred_element_type=F32)


def dot_nt(left, right):
    return lax.dot_general(left, right, (((1,), (1,)), ((), ())), preferred_element_type=F32)


def tile(n):
    return pl.ds(pl.multiple_of(n * 256, 256), 256)


def layer_kernel(
    n_dp,
    x_in, cot_in, wq_in, wk_in, wv_in, wo_in, wup_in, wdn_in,
    len_in, qd_in, vd_in, qu_in, vu_in, qb_in, vb_in, ub_in, *rest
):
    small_from = (len_in, qd_in, vd_in, qu_in, vu_in, qb_in, vb_in, ub_in, *rest[:6])
    rest = rest[6:]
    (
        out_ref, dx_ref, lora_ref,
        wqkv, wo, wup, wdn, small, lora_q, lora_v, vec_in, down_in,
        xwin, uwin, qwin, kwin, vwin, dowin, stwin, mask,
        att, attf, stat, midb, norm1, stat1, hid, gelp, acc, gffn, gbuf, dq, dk_acc, dv_acc, dkv,
        lsend, lrecv1, lrecv2,
        lsem, ssem, rsem,
        *small_to,
    ) = rest
    len_in, qd_in, vd_in, qu_in, vu_in, qb_in, vb_in, ub_in, *vec_refs = small_to
    rows = x_in.shape[0]
    width = x_in.shape[1]
    pairs = width // LANES
    dp, t = lax.axis_index("dp"), lax.axis_index("tensor")
    member = lax.rem(dp, GROUP)
    core = lax.rem(member, 2)
    yx = member // 2
    yx_x = yx + 1 - 2 * lax.rem(yx, 2)
    yx_y = yx + 2 - 4 * (yx // 2)
    yx_d = 3 - yx
    x_dev = (dp + 2 * (yx_x - yx), t)
    y_dev = (dp + 2 * (yx_y - yx), t)
    c_dev = (dp + 1 - 2 * core, t)

    def shard(a):
        first = jnp.where(t == 0, 1, t - 1)
        second = jnp.where(t == 0, 2, jnp.where(t == 3, 1, t + 1))
        third = jnp.where(t < 2, 3, 0)
        return jnp.where(a == 1, first, jnp.where(a == 2, second, third))

    barrier = pltpu.get_barrier_semaphore()
    for d in range(1, 4):
        pl.semaphore_signal(barrier, inc=1, device_id=(dp, lax.rem(t + d, 4)), device_id_type=MESH)
    for d in range(1, n_dp):
        pl.semaphore_signal(barrier, inc=1, device_id=(lax.rem(dp + d, n_dp), t), device_id_type=MESH)

    count = {"send": 0, "recv": 0, "local": 0}
    pending = {}

    def alloc(kind, n):
        first = count[kind]
        count[kind] += n
        return first

    def when(pred, fn):
        if pred is None:
            fn()
        else:
            pl.when(pred)(fn)

    def remote(src, dst, recv, dev, pred=None):
        slot = alloc("send", 1) % ssem.shape[0]
        if slot in pending:
            before, copy = pending[slot]
            when(before, copy.wait_send)
        copy = pltpu.make_async_remote_copy(
            src_ref=src, dst_ref=dst, send_sem=ssem.at[slot], recv_sem=rsem.at[recv],
            device_id=dev, device_id_type=MESH,
        )
        when(pred, copy.start)
        pending[slot] = (pred, copy)

    def arrived(dst, recv, pred=None):
        copy = pltpu.make_async_remote_copy(
            src_ref=dst, dst_ref=dst, send_sem=ssem.at[0], recv_sem=rsem.at[recv],
            device_id=(dp, t), device_id_type=MESH,
        )
        when(pred, copy.wait_recv)

    def local(src, dst):
        copy = pltpu.make_async_copy(src, dst, lsem.at[alloc("local", 1)])
        copy.start()
        return copy

    ld_small = [local(a, b) for a, b in zip(small_from, small_to)]
    ld_qkv = [
        local(w, wqkv.at[t, :, :, :, pl.ds(256 * i, 256)]) for i, w in enumerate((wq_in, wk_in, wv_in))
    ]
    ld_x = [local(x_in, xwin.at[2])]
    ld_up = [local(wup_in, wup.at[t])]
    ld_o = [local(wo_in, wo.at[t])]
    ld_dn = [local(wdn_in, wdn.at[t])]
    ld_cot = [local(cot_in, gffn)]

    def done(copies):
        while copies:
            copies.pop().wait()

    class Chunk:
        def __init__(self, ref, first, size, loads):
            self.ref, self.first, self.size, self.loads = ref, first, size, loads
            self.zr = alloc("recv", 4)
            self.xr, self.yr, self.dr, self.cr = (alloc("recv", 3) - 1 for _ in range(4))

        def region(self, s, place, lo=0, size=None):
            return self.ref.at[s, place, core, pl.ds(self.first + lo, size or self.size), :]

        def send(self):
            done(self.loads)
            own = self.region(t, yx)
            remote(own, own, self.zr + t, (dp, jnp.minimum(t + 1, 3)), t < 3)
            remote(own, own, self.zr + t, (dp, jnp.maximum(t - 1, 0)), t > 0)

        def stage0(self, a):
            s = shard(a)
            own = self.region(s, yx)
            arrived(own, self.zr + s)
            onward = jnp.where(s < t, t + 1, t - 1)
            remote(
                own, own, self.zr + s, (dp, jnp.clip(onward, 0, 3)),
                jnp.logical_and(onward >= 0, onward <= 3),
            )
            remote(own, own, self.xr + a, x_dev)
            remote(own, own, self.yr + a, y_dev)

        def stage1(self, a):
            s, half = shard(a), self.size // 2
            arrived(self.region(s, yx_x), self.xr + a)
            part = self.region(s, yx_x, 0, half)
            remote(part, part, self.dr + a, y_dev)
            arrived(self.region(s, yx_y), self.yr + a)
            part = self.region(s, yx_y, half, half)
            remote(part, part, self.dr + a, x_dev)

        def stage2(self, a):
            s = shard(a)
            arrived(self.region(s, yx_d), self.dr + a)
            four = self.ref.at[s, :, core, pl.ds(self.first, self.size), :]
            remote(four, four, self.cr + a, c_dev)

        def stage3(self, a):
            s = shard(a)
            arrived(self.ref.at[s, :, 1 - core, pl.ds(self.first, self.size), :], self.cr + a)

    upward, downward = (dp, jnp.minimum(t + 1, 3)), (dp, jnp.maximum(t - 1, 0))
    after, before = (jnp.minimum(dp + 1, n_dp - 1), t), (jnp.maximum(dp - 1, 0), t)
    not_last, not_first = dp < n_dp - 1, dp > 0

    class Exchange:
        def __init__(self, ref, first, size):
            self.ref, self.low, self.size = ref, first, size
            self.base = alloc("recv", 6)

        def at(self, slot):
            return self.ref.at[slot, pl.ds(self.low, self.size), :]

        def go(self, src, dst, dev, pred):
            remote(self.at(src), self.at(dst), self.base + dst, dev, pred)

        def get(self, slot, pred):
            arrived(self.at(slot), self.base + slot, pred)

        def first(self):
            self.go(2, 1, upward, t < 3)
            self.go(2, 3, downward, t > 0)
            self.go(2, 5, after, jnp.logical_and(t == 3, not_last))
            self.go(2, 5, before, jnp.logical_and(t == 0, not_first))

        def neighbours(self):
            self.get(1, t >= 1)
            self.get(3, t <= 2)
            self.go(1, 0, upward, t == 2)
            self.go(3, 4, downward, t == 1)

        def chain1(self):
            self.get(5, jnp.logical_and(t == 3, not_first))
            self.get(5, jnp.logical_and(t == 0, not_last))
            self.go(5, 5, downward, jnp.logical_and(t == 3, not_first))
            self.go(5, 5, upward, jnp.logical_and(t == 0, not_last))

        def chain2(self):
            self.get(5, jnp.logical_and(t == 2, not_first))
            self.get(5, jnp.logical_and(t == 1, not_last))
            self.go(5, 0, downward, jnp.logical_and(t == 2, not_first))
            self.go(5, 4, upward, jnp.logical_and(t == 1, not_last))
            self.go(1, 0, upward, t == 1)
            self.go(3, 4, downward, t == 2)

        def ends(self):
            self.get(4, t == 0)
            self.get(0, t == 3)
            self.go(4, 0, after, jnp.logical_and(t == 0, not_last))
            self.go(0, 4, before, jnp.logical_and(t == 3, not_first))

        def chain3(self):
            self.get(0, jnp.logical_and(t == 1, not_first))
            self.get(4, jnp.logical_and(t == 2, not_last))
            self.go(0, 1, downward, jnp.logical_and(t == 1, not_first))
            self.go(4, 3, upward, jnp.logical_and(t == 2, not_last))

        def third(self):
            self.get(0, jnp.logical_and(t == 0, not_first))
            self.get(4, jnp.logical_and(t == 3, not_last))

        def last(self):
            self.get(1, jnp.logical_and(t == 0, not_first))
            self.get(3, jnp.logical_and(t == 3, not_last))
            self.get(4, t == 1)
            self.get(0, t == 2)

    lane = lax.broadcasted_iota(jnp.int32, (1, LANES), 1)
    first_half = lane < HD

    def vec(i):
        return vec_in[i : i + 1, :]

    def halves(block):
        zero = jnp.zeros_like(block)
        return jnp.where(first_half, block, zero), jnp.where(first_half, zero, block)

    def clear(ref):
        def fill(pred, slot):
            @pl.when(pred)
            def _():
                ref[slot] = jnp.zeros(ref.shape[1:], ref.dtype)

        fill(jnp.logical_and(dp == 0, t <= 1), 0)
        fill(jnp.logical_and(dp == 0, t == 0), 1)
        fill(jnp.logical_and(dp == n_dp - 1, t >= 2), 4)
        fill(jnp.logical_and(dp == n_dp - 1, t == 3), 3)

    def adapter(w):
        uwin[w] = dot_nt(xwin[w], down_in[...]).astype(BF16)

    def proj(w, pos, s):
        y = dot(xwin[w], wqkv[s].reshape(width, 3 * 256))
        u = uwin[w]
        place = (tile(pos), tile(s))
        q = y[:, :256] + dot(u, lora_q[s]) + small[s, 16:17, :]
        qwin[place] = (q * (1.0 / math.sqrt(HD))).astype(BF16)
        kwin[place] = y[:, 256:512].astype(BF16)
        v = y[:, 512:] + dot(u, lora_v[s]) + small[s, 17:18, :]
        vwin[place] = v.astype(BF16)

    def proj_all(w, pos):
        adapter(w)

        @pl.loop(0, 4)
        def _(s):
            proj(w, pos, s)

    def loop_pairs(lo, hi, body, unroll=1):
        @pl.loop(lo, hi, unroll=unroll)
        def _(p):
            body(p, pl.ds(pl.multiple_of(p * LANES, LANES), LANES))

    def column(index):
        return jnp.sum(jnp.where(lane == index, stat[...], 0.0), axis=1, keepdims=True)

    def attend(lo, hi):
        begin, end = lo * 256, hi * 256

        def body(p, cols):
            q_heads = halves(qwin[tile(1), cols])
            k, v = kwin[begin:end, cols], vwin[begin:end, cols]
            before, outs, found = attf[:, cols], [], stat[...]
            for i in range(2):
                s = dot_nt(q_heads[i], k) + mask[:, begin:end]
                top = jnp.max(s, axis=1, keepdims=True)
                if lo:
                    old = column(2 * p + i)
                    top = jnp.maximum(top, old)
                e = jnp.exp(s - top)
                total = jnp.sum(e, axis=1, keepdims=True)
                o = dot(e.astype(BF16), v)
                if lo:
                    alpha = jnp.exp(old - top)
                    total = total + column(16 + 2 * p + i) * alpha
                    o = o + before * alpha
                if hi == 5:
                    o = o * (1.0 / total)
                    top = top + jnp.log(total)
                outs.append(o)
                found = jnp.where(lane == 2 * p + i, top, jnp.where(lane == 16 + 2 * p + i, total, found))
            o = jnp.where(first_half, outs[0], outs[1])
            attf[:, cols] = o
            if hi == 5:
                att[:, cols] = o.astype(BF16)
            stat[...] = found

        return body

    def after_attention():
        @pl.loop(0, 4, unroll=4)
        def _(n):
            acc[:, tile(n)] = dot(att[...], wo[:, :, :, :, tile(n)].reshape(width, 256))

        z = xwin[2].astype(F32) + acc[...] + vec(0)
        centre = z - jnp.mean(z, axis=1, keepdims=True)
        r = lax.rsqrt(jnp.mean(centre * centre, axis=1, keepdims=True) + NORM_EPS)
        n1 = centre * r
        norm1[...] = n1
        stat1[...] = jnp.broadcast_to(r, stat1.shape)
        m = n1 * vec(1) + vec(2)
        midb[...] = m.astype(BF16)
        acc[...] = m + vec(3)

    def up(s):
        @pl.loop(0, 4, unroll=4)
        def _(n):
            b = dot(midb[...], wup[s, :, :, :, tile(n)].reshape(width, 256)) + small[s, pl.ds(18 + n, 1), :]
            cdf = 0.5 + 0.5 * lax.erf(b * (1.0 / math.sqrt(2.0)))
            hid[s, :, tile(n)] = (b * cdf).astype(BF16)
            gelp[s, :, tile(n)] = cdf + b * jnp.exp(-0.5 * b * b) * (1.0 / math.sqrt(2.0 * math.pi))

    def down(s):
        @pl.loop(0, 4, unroll=4)
        def _(n):
            acc[:, tile(n)] += dot(hid[s], wdn[s, :, :, :, tile(n)].reshape(width, 256))

    def second_norm():
        z = acc[...]
        centre = z - jnp.mean(z, axis=1, keepdims=True)
        r = lax.rsqrt(jnp.mean(centre * centre, axis=1, keepdims=True) + NORM_EPS)
        n2 = centre * r
        midb[...] = (n2 * vec(4) + vec(5)).astype(BF16)
        g = gffn[...].astype(F32) * vec(4)
        g = r * (g - jnp.mean(g, axis=1, keepdims=True) - n2 * jnp.mean(g * n2, axis=1, keepdims=True))
        acc[...] = g
        gffn[...] = g.astype(BF16)

    def ffn_back(s):
        @pl.loop(0, 4, unroll=4)
        def _(n):
            toward = dot_nt(gffn[...], wdn[s, n].reshape(256, width))
            gbuf[:, tile(n)] = (toward * gelp[s, :, tile(n)]).astype(BF16)

        @pl.loop(0, 4, unroll=4)
        def _(n):
            acc[:, tile(n)] += dot_nt(gbuf[...], wup[s, n].reshape(256, width))

    def first_norm_back():
        g = acc[...] * vec(1)
        n1 = norm1[...]
        g = g - jnp.mean(g, axis=1, keepdims=True) - n1 * jnp.mean(g * n1, axis=1, keepdims=True)
        g = stat1[:, 0:1] * g
        acc[...] = g
        gffn[...] = g.astype(BF16)

        @pl.loop(0, 4, unroll=4)
        def _(s):
            dowin[2, :, tile(s)] = dot_nt(gffn[...], wo[s].reshape(256, width)).astype(BF16)

        product = dowin[2].astype(F32) * attf[...]
        high = product.astype(BF16)
        low = (product - high.astype(F32)).astype(BF16)
        at_row = lax.broadcasted_iota(jnp.int32, (width, LANES), 0) // HD + 16
        at_lane = lax.broadcasted_iota(jnp.int32, (width, LANES), 1)
        pick = (at_row == at_lane).astype(F32).astype(BF16)
        delta = dot(high, pick) + dot(low, pick)
        both = jnp.where(lane < 16, stat[...], delta)
        stat[...] = both
        stwin[2] = both.T[0:32]

    def pass_queries(p, cols):
        q_heads, do_heads = halves(qwin[tile(1), cols]), halves(dowin[2, :, cols])
        k, v = kwin[:, cols], vwin[:, cols]
        parts = []
        for i in range(2):
            prob = jnp.exp(dot_nt(q_heads[i], k) + mask[...] - column(2 * p + i))
            ds = prob * (dot_nt(do_heads[i], v) - column(16 + 2 * p + i))
            parts.append(dot(ds.astype(BF16), k))
        dq[:, cols] = (jnp.where(first_half, parts[0], parts[1]) * (1.0 / math.sqrt(HD))).astype(BF16)

    def pass_keys(names, at, end, first=False, keys=True, values=True, unroll=1):
        slots = [blocks[name][0] for name in names]
        begin = blocks[names[0]][1] * rows
        window = slice(begin, begin + len(names) * rows)

        def line(index):
            parts = [stwin[w, pl.ds(index, 1), :] for w in slots]
            return parts[0] if len(parts) == 1 else jnp.concatenate(parts, axis=1)

        def body(p, cols):
            k_heads, v_heads = halves(kwin[tile(1), cols]), halves(vwin[tile(1), cols])
            q, do = qwin[window, cols], [dowin[w, :, cols] for w in slots]
            do = do[0] if len(do) == 1 else jnp.concatenate(do, axis=0)
            if len(slots) == 1:
                scores = dot_nt(jnp.concatenate(k_heads, axis=0), q)
                scores = [scores[:256], scores[256:]]
                if keys:
                    grads = dot_nt(jnp.concatenate(v_heads, axis=0), do)
                    grads = [grads[:256], grads[256:]]
            else:
                scores = [dot_nt(k, q) for k in k_heads]
                grads = [dot_nt(v, do) for v in v_heads]
            probs, ds = [], []
            for i in range(2):
                prob = jnp.exp(scores[i] + mask[:, window] - line(2 * p + i))
                if keys:
                    ds.append((prob * (grads[i] - line(16 + 2 * p + i))).astype(BF16))
                probs.append(prob.astype(BF16))
            for total, lefts, right, wanted in ((dk_acc, ds, q, keys), (dv_acc, probs, do, values)):
                if wanted:
                    if len(slots) == 1:
                        both = dot(jnp.concatenate(lefts, axis=0), right)
                        both = jnp.where(first_half, both[:256], both[256:])
                    else:
                        both = jnp.where(first_half, dot(lefts[0], right), dot(lefts[1], right))
                    total[:, cols] = both if first else total[:, cols] + both

        loop_pairs(at, end, body, unroll)

    def lora_partial():
        u = uwin[2].astype(F32).T[0:16].astype(BF16)
        is_query = lax.broadcasted_iota(jnp.int32, (16, 1), 0) < 8
        for s in range(4):
            cols = slice(256 * s, 256 * s + 256)
            both = jnp.where(is_query, dot(u, dq[:, cols]), dot(u, dkv[1, :, cols]))
            lsend[s] = both

    def input_gradient():
        gu = jnp.zeros((rows, LANES), F32)
        for s in range(4):
            cols = slice(256 * s, 256 * s + 256)
            gu = gu + dot_nt(dq[:, cols], lora_q[s]) + dot_nt(dkv[1, :, cols], lora_v[s])
        gu = gu.astype(BF16)

        @pl.loop(0, 4, unroll=4)
        def _(n):
            total = acc[:, tile(n)] + dot(gu, down_in[:, tile(n)])
            for s in range(4):
                cols = slice(256 * s, 256 * s + 256)
                three = jnp.concatenate([dq[:, cols], dkv[0, :, cols], dkv[1, :, cols]], axis=1)
                total = total + dot_nt(three, wqkv[s, n].reshape(256, 3 * 256))
            att[:, tile(n)] = total.astype(BF16)

    def chunk(ref, first, size, loads):
        return Chunk(ref, first, size, loads)

    qkv0, qkv1 = chunk(wqkv, 0, 64, ld_qkv), chunk(wqkv, 64, 64, ld_qkv)
    up0, up1 = chunk(wup, 0, 64, ld_up), chunk(wup, 64, 64, ld_up)
    dn0, dn1 = chunk(wdn, 0, 64, ld_dn), chunk(wdn, 64, 64, ld_dn)
    o0 = chunk(wo, 0, 32, ld_o)
    quarter = rows // 4
    tok = [Exchange(xwin, i * quarter, quarter) for i in range(4)]
    small_base = alloc("recv", 4)
    wide = [Exchange(dowin, i * quarter, quarter) for i in range(4)]
    narrow = Exchange(stwin, 0, 32)
    lora1 = alloc("recv", 4)
    lora2 = alloc("recv", n_dp)

    clear(xwin)
    done(ld_small)
    for i in range(8):
        cols = slice(LANES * i, LANES * i + LANES)
        for j, ref in enumerate(vec_refs):
            vec_in[j : j + 1, cols] = ref[i : i + 1, :].astype(F32)
    own_small = [2.0 * qu_in[...].astype(F32), 2.0 * vu_in[...].astype(F32)]
    small[t, 0:8, :] = own_small[0]
    small[t, 8:16, :] = own_small[1]
    for i in range(2):
        cols = slice(LANES * i, LANES * i + LANES)
        small[t, 16:17, cols] = qb_in[i : i + 1, :].astype(F32)
        small[t, 17:18, cols] = vb_in[i : i + 1, :].astype(F32)
        for j in range(4):
            small[t, 18 + j : 19 + j, cols] = ub_in[2 * j + i : 2 * j + i + 1, :].astype(F32)
    small[t, 22:24, :] = jnp.zeros((2, 256), F32)
    maps = [qd_in[...].astype(F32), vd_in[...].astype(F32), jnp.zeros((LANES - 16, width), F32)]
    down_in[...] = jnp.concatenate(maps, axis=0).astype(BF16)
    pl.semaphore_wait(barrier, 3 + n_dp - 1)
    done(ld_x)
    for d in range(1, 4):
        remote(small.at[t], small.at[t], small_base + t, (dp, lax.rem(t + d, 4)))

    near = jnp.where(t < 3, 3, 1)
    second = jnp.where(lax.rem(t, 2) == 0, 4, 0)
    third = jnp.where(t == 0, 0, jnp.where(t == 3, 4, 1))
    final = jnp.where(t == 0, 1, jnp.where(t == 1, 4, jnp.where(t == 2, 0, 3)))
    blocks = {"n": (near, 0), "2": (2, 1), "s": (second, 2), "t": (third, 3), "l": (final, 4)}
    named = {"q0": qkv0, "q1": qkv1, "u0": up0, "u1": up1, "d0": dn0, "d1": dn1, "o": o0}
    def setup():
        lengths = len_in[...]
        docs = lengths.shape[0] * LANES
        high, low = lengths // 256, lax.rem(lengths, 256)
        upto = (
            lax.broadcasted_iota(jnp.int32, (LANES, LANES), 0)
            <= lax.broadcasted_iota(jnp.int32, (LANES, LANES), 1)
        ).astype(F32).astype(BF16)

        def summed(part):
            return dot(part.astype(F32).astype(BF16), upto)

        ends = 256.0 * summed(high) + summed(low)
        window = mask.shape[1]
        first = (dp * 4 + t) * rows - MAXLEN
        spot = lax.broadcasted_iota(jnp.int32, (1, window), 1)
        place = spot // rows
        where = place
        for slot, nth_place in blocks.values():
            where = jnp.where(place == nth_place, slot, where)
        position = first + where * rows + lax.rem(spot, rows)
        at = position.astype(F32)
        passed = jnp.zeros((1, window), F32)
        before = jnp.zeros((1, 1), F32)
        for r in range(lengths.shape[0]):
            end = ends[r : r + 1, :] + before
            before = end[:, LANES - 1 :]
            column = jnp.broadcast_to(end, (LANES, LANES)).T[:, 0:1]
            passed = passed + jnp.sum((column <= at).astype(F32), axis=0, keepdims=True)
        inside = jnp.logical_and(position >= 0, passed < docs)
        ids = jnp.where(inside, passed, -1.0)
        own = jnp.broadcast_to(ids[:, rows : 2 * rows], (LANES, rows)).T[:, 0:1]
        mask[...] = jnp.where(own == ids, 0.0, MASKED)
        stat[...] = jnp.zeros(stat.shape, F32)

    def small_ready():
        for d in range(1, 4):
            peer = lax.rem(t + d, 4)
            arrived(small.at[peer], small_base + peer)
        none = jnp.zeros((8, 256), F32)
        lora_q[:, 16:, :] = jnp.zeros((4, LANES - 16, 256), BF16)
        lora_v[:, 16:, :] = jnp.zeros((4, LANES - 16, 256), BF16)
        for s in range(4):
            lora_q[s, 0:16, :] = jnp.concatenate([small[s, 0:8, :], none], axis=0).astype(BF16)
            lora_v[s, 0:16, :] = jnp.concatenate([none, small[s, 8:16, :]], axis=0).astype(BF16)


    def part(a):
        return t if a == 0 else shard(a)

    for item in PLAN:
        kind, rest = item[0], item[1:]
        if kind == "+":
            named[rest].send()
        elif kind in "0123":
            getattr(named[rest[:-1]], "stage" + kind)(int(rest[-1]))
        elif kind in STEPS:
            getattr(tok[int(rest)], STEPS[kind])()
        elif item == "P20":
            setup()
            small_ready()
            adapter(2)
            done(ld_qkv)
            proj(2, 1, t)
        elif item == "P2":

            @pl.loop(1, 4)
            def _(a):
                proj(2, 1, shard(a))

        elif kind == "P":
            proj_all(*blocks[rest])
        elif kind == "A":
            at, lo, hi = (int(i) for i in rest)
            loop_pairs(at, at + 4, attend(lo, hi))
        elif kind == "M":
            done(ld_o)
            after_attention()
        elif kind == "U":
            done(ld_up)
            up(part(int(rest)))
        elif kind == "D":
            done(ld_dn)
            down(part(int(rest)))
    for copies in (ld_qkv, ld_o, ld_up, ld_dn):
        done(copies)

    done(ld_cot)
    second_norm()
    out_copy = local(midb, out_ref)
    clear(dowin)
    clear(stwin)

    @pl.loop(0, 4)
    def _(s):
        ffn_back(s)

    first_norm_back()

    def swap(step, i):
        for e in [wide[i]] + ([narrow] if i == 0 else []):
            getattr(e, step)()

    for item in PLAN_BACK:
        kind, rest = item[0], item[1:]
        if kind in STEPS:
            swap(STEPS[kind], int(rest))
        elif kind == "Q":
            loop_pairs(int(rest), int(rest) + 2, pass_queries)
        elif kind == "K":
            names, at = rest[:2], int(rest[2])
            pass_keys(names, at, at + 4, first=names == "n2")
        elif kind == "V":
            pass_keys("l", 0, pairs, keys=False, unroll=2)
        elif kind == "G":
            dkv[1] = dv_acc[...].astype(BF16)
            lora_partial()
            for d in range(1, 4):
                peer = lax.rem(t + d, 4)
                remote(lsend.at[peer], lrecv1.at[t], lora1 + t, (dp, peer))
            lrecv1[t] = lsend[t]
        elif kind == "L":
            pass_keys("l", 0, pairs, values=False, unroll=2)
            dkv[0] = dk_acc[...].astype(BF16)
        elif kind == "H":
            for d in range(1, 4):
                peer = lax.rem(t + d, 4)
                arrived(lrecv1.at[peer], lora1 + peer)
            lrecv2[dp] = 2.0 * ((lrecv1[0] + lrecv1[1]) + (lrecv1[2] + lrecv1[3]))
            for d in range(1, n_dp):
                remote(lrecv2.at[dp], lrecv2.at[dp], lora2 + dp, (lax.rem(dp + d, n_dp), t))
        elif kind == "I":
            input_gradient()
    dx_copy = local(att, dx_ref)
    for d in range(1, n_dp):
        peer = lax.rem(dp + d, n_dp)
        arrived(lrecv2.at[peer], lora2 + peer)
    total = lrecv2[0]
    for i in range(1, n_dp):
        total = total + lrecv2[i]
    lora_ref[...] = total
    dx_copy.wait()
    out_copy.wait()
    for pred, copy in pending.values():
        when(pred, copy.wait_send)
    assert count["recv"] <= rsem.shape[0] and count["local"] <= lsem.shape[0]


def hand_over(out, grad, lora, out_to, grad_to, query_to, value_to, out_at, grad_at, lora_at, sems):
    rows = out.shape[0] // 2
    halves = [pl.ds(i * rows, rows) for i in range(2)]
    loads = [(lora, lora_at)]
    stores = [[(lora_at.at[0:8], query_to), (lora_at.at[8:16], value_to)]]
    for source, at, to in ((out, out_at, out_to), (grad, grad_at, grad_to)):
        for half in halves:
            loads.append((source.at[half], at.at[half]))
            stores.append([(at.at[half], to.at[half])])
    copies = [pltpu.make_async_copy(a, b, sems.at[i]) for i, (a, b) in enumerate(loads)]
    for copy in copies:
        copy.start()
    moved = []
    for copy, pairs in zip(copies, stores):
        copy.wait()
        for a, b in pairs:
            moved.append(pltpu.make_async_copy(a, b, sems.at[len(copies) + len(moved)]))
            moved[-1].start()
    for copy in moved:
        copy.wait()


def shards(
    tokens, document_lengths, query_proj_weight, query_proj_bias, key_proj_weight, value_proj_weight,
    value_proj_bias, query_adapter_down, value_adapter_down, query_adapter_up, value_adapter_up,
    attention_out_weight, attention_out_bias, attention_norm_gain, attention_norm_bias, up_proj_weight,
    up_proj_bias, down_proj_weight, down_proj_bias, feedforward_norm_gain, feedforward_norm_bias, cotangent,
):
    rows, width = tokens.shape
    n_dp = lax.axis_size("dp")
    window = rows + 2 * MAXLEN

    def fold(vector):
        return vector.reshape(vector.shape[0] // LANES, LANES)

    def cut(weight):
        return weight.reshape(4, 2, weight.shape[0] // GROUP, weight.shape[1])

    def vmem(shape, dtype):
        return pltpu.VMEM(shape, dtype)

    small_arrays = (
        fold(document_lengths), query_adapter_down.T, value_adapter_down.T, query_adapter_up, value_adapter_up,
        fold(query_proj_bias), fold(value_proj_bias), fold(up_proj_bias), fold(attention_out_bias),
        fold(attention_norm_gain), fold(attention_norm_bias), fold(down_proj_bias), fold(feedforward_norm_gain),
        fold(feedforward_norm_bias),
    )
    any_spec = pl.BlockSpec(memory_space=pl.ANY)
    vmem_spec = pl.BlockSpec(memory_space=pltpu.VMEM)
    full = (rows, width)
    rank = query_adapter_up.shape[0]
    call = pl.pallas_call(
        lambda *refs: layer_kernel(n_dp, *refs),
        out_shape=(
            jax.ShapeDtypeStruct(full, BF16),
            jax.ShapeDtypeStruct(full, BF16),
            jax.ShapeDtypeStruct((16, 256), F32),
        ),
        in_specs=[any_spec] * 22,
        out_specs=(any_spec, any_spec, vmem_spec),
        scratch_shapes=[
            vmem((4, 4, 2, 128, 768), BF16),
            vmem((4, 4, 2, 32, 1024), BF16),
            vmem((4, 4, 2, 128, 1024), BF16),
            vmem((4, 4, 2, 128, 1024), BF16),
            vmem((4, 24, 256), F32),
            vmem((4, 128, 256), BF16),
            vmem((4, 128, 256), BF16),
            vmem((8, width), F32),
            vmem((LANES, width), BF16),
            vmem((6, rows, width), BF16),
            vmem((5, rows, LANES), BF16),
            vmem((window, width), BF16),
            vmem((window, width), BF16),
            vmem((window, width), BF16),
            vmem((6, rows, width), BF16),
            vmem((6, 32, rows), F32),
            vmem((rows, window), F32),
            vmem(full, BF16),
            vmem(full, F32),
            vmem((rows, LANES), F32),
            vmem(full, BF16),
            vmem(full, F32),
            vmem((rows, LANES), F32),
            vmem((4, rows, width), BF16),
            vmem((4, rows, width), F32),
            vmem(full, F32),
            vmem(full, BF16),
            vmem(full, BF16),
            vmem(full, BF16),
            vmem(full, F32),
            vmem(full, F32),
            vmem((2, rows, width), BF16),
            vmem((4, 16, 256), F32),
            vmem((4, 16, 256), F32),
            vmem((n_dp, 16, 256), F32),
            pltpu.SemaphoreType.DMA((26,)),
            pltpu.SemaphoreType.DMA((48,)),
            pltpu.SemaphoreType.DMA((174 + n_dp,)),
        ]
        + [vmem(a.shape, a.dtype) for a in small_arrays],
        compiler_params=pltpu.CompilerParams(
            collective_id=0, has_side_effects=True, vmem_limit_bytes=63 * 2**20
        ),
        name="layer",
    )
    out, grad, lora = call(
        tokens, cotangent, cut(query_proj_weight), cut(key_proj_weight), cut(value_proj_weight),
        cut(attention_out_weight), cut(up_proj_weight), cut(down_proj_weight), *small_arrays,
    )
    lora_shape = jax.ShapeDtypeStruct((rank, 256), F32)
    return pl.pallas_call(
        hand_over,
        out_shape=(out, grad, lora_shape, lora_shape),
        in_specs=[any_spec] * 3,
        out_specs=(any_spec,) * 4,
        scratch_shapes=[
            vmem(full, BF16), vmem(full, BF16), vmem((2 * rank, 256), F32), pltpu.SemaphoreType.DMA((11,))
        ],
        name="hand_over",
    )(out, grad, lora)


def solution(mesh):
    whole, columns = P(), P(None, "tensor")
    stream = P(("dp", "tensor"), None)
    return jax.shard_map(
        shards,
        mesh=mesh,
        in_specs=(
            stream, whole, columns, P("tensor"), columns, columns, P("tensor"), whole, whole, columns, columns,
            P("tensor", None), whole, whole, whole, columns, P("tensor"), P("tensor", None), whole, whole, whole,
            stream,
        ),
        out_specs=(stream, stream, columns, columns),
        check_vma=False,
    )
```

profile of v0, /device:TPU:2, one launch (start us, length us, event | category | flops | bytes accessed | tf_op | source)
XLA Modules:
  0.0 176.2 jit_solution(2596510451912924697)
XLA Ops:
  0.6 173.4 %layer.1 = (bf16[256,1024]{1,0:T(8,128)(2,1)}, bf16[256,1024]{1,0:T(8,128)(2,1)}, f32[16,256]{1,0:T(8,128)}) custom-call(bf16[256,1024]{1,0:T(8,128)(2,1)} %refs_0_.1, bf16[256,1024]{1,0:T(8,128)(2,1)} %refs_1_.1, bf16[4,2,128,256]{3,2,1,0:T(8,128)(2,1)} %bitcast.20, bf16[4,2,128,256]{3,2,1,0:T(8,128)(2,1)} %bitcast.21, bf16[4,2,128,256]{3,2,1,0:T(8,128)(2,1)} %bitcast.22, ...), custom_call_target="tpu_custom_call" | custom-call | tf_op jit(solution)/shard_map/layer/pallas_call | solution.py:785
  174.0 2.0 %hand_over.1 = (bf16[256,1024]{1,0:T(8,128)(2,1)}, bf16[256,1024]{1,0:T(8,128)(2,1)}, f32[8,256]{1,0:T(8,128)}, f32[8,256]{1,0:T(8,128)}) custom-call(bf16[256,1024]{1,0:T(8,128)(2,1)} %get-tuple-element.7.out, bf16[256,1024]{1,0:T(8,128)(2,1)} %get-tuple-element.8.grad, f32[16,256]{1,0:T(8,128)} %get-tuple-element.9.lora), custom_call_target="tpu_custom_call" | custom-call | tf_op jit(solution)/shard_map/hand_over/pallas_call | solution.py:790
where the time goes:
time: 178 us; the launch traced here: 176 us
  Pallas kernels  175 us (98%)
    pallas_call x1, Pallas kernels, shards(): call(tokens, cotangent, cut(query_proj_weight), cut(key_proj_weight), cut...  173 us

commit v1 on v0

--- a/solution.py
+++ b/solution.py
@@ -18,21 +18,21 @@
     "S": "first", "n": "neighbours", "c": "chain1", "C": "chain2", "x": "ends", "y": "chain3", "t": "third", "l": "last",
 }
 PLAN_BACK = (
-    "S2", "S0", "n2", "c0", "S1", "Q2", "c2", "c1", "n0", "S3", "C0", "Q6", "n1", "x2", "c3", "y0", "C2", "Q0",
-    "C1", "x0", "n3", "x1", "t2", "y2", "Kn24", "C3", "Q4", "y1", "t0", "x3", "l0", "Kn20", "t3", "t1", "l1", "l2",
-    "y3", "Kst0", "Kst4", "l3", "V", "G", "L", "H", "I", "J",
+    "S1", "S0", "c1", "Q2", "n1", "S3", "c0", "Q0", "S2", "C1", "Q6", "n0", "n3", "Q4", "C0", "G", "x0", "n2", "c2",
+    "Kn20", "c3", "y0", "y1", "x1", "C2", "x3", "i", "Kn24", "t0", "t1", "C3", "l0", "x2", "y2", "Kx0", "H", "t2",
+    "l1", "t3", "l2", "y3", "Kx1", "l3", "Kl", "I", "J",
 )
 PLAN = (
-    "+q1", "+q0", "S2", "0q11", "0q01", "1q11", "0q12", "0q02", "2q11", "1q01", "S3", "0q03", "+o", "+u0", "c3",
-    "2q01", "1q02", "1q03", "0o1", "0o2", "0q13", "+u1", "0u01", "1q13", "+d1", "0u11", "S1", "2q13", "S0", "1u01",
-    "P20", "1q12", "2q03", "0u02", "0u12", "3q11", "n2", "2q02", "n3", "c1", "C3", "3q01", "3q13", "2q12", "1u02",
-    "1u11", "3q02", "2u01", "3q12", "3q03", "n1", "c2", "1o1", "n0", "x3", "+d0", "P2", "c0", "1o2", "x2", "1u12",
-    "C1", "2u11", "Pn", "x1", "x0", "t2", "2o1", "2o2", "0o3", "t0", "0d11", "A002", "t1", "0u03", "3u01", "1o3",
-    "0d01", "2u12", "3o1", "C2", "t3", "2u02", "3o2", "Pt", "0d02", "3u11", "y3", "2o3", "A402", "C0", "0d12",
-    "0u13", "l3", "3o3", "y0", "y2", "y1", "Ps", "1u03", "l0", "1d11", "A024", "A424", "l2", "1d01", "1u13", "l1",
-    "2u03", "1d02", "0d13", "2d11", "Pl", "A445", "1d12", "2d01", "0d03", "2d02", "2u13", "A045", "3u12", "M", "U1",
-    "3u02", "1d13", "2d12", "3u13", "U0", "3d01", "1d03", "3d11", "D1", "3d12", "2d13", "U2", "3d02", "3u03",
-    "2d03", "U3", "D2", "D0", "3d03", "3d13", "D3",
+    "+q1", "+q0", "+u0", "S3", "0q11", "0q01", "1q11", "0u01", "1q01", "0q12", "0q02", "S2", "c3", "2q01", "1u01",
+    "1q12", "0u02", "S0", "2q11", "0q03", "0q13", "+o", "+u1", "S1", "n0", "1q03", "1q13", "1u02", "c2", "2q03",
+    "0o1", "1q02", "0u11", "2q12", "2u02", "0o2", "x0", "c1", "+d0", "2q13", "1o1", "P20", "0u12", "2q02", "0o3",
+    "n3", "3q11", "C3", "3q12", "3u02", "3q03", "n2", "3q13", "3q02", "1o2", "t0", "3q01", "n1", "x3", "P2", "C2",
+    "2u01", "1u12", "x2", "1u11", "c0", "1o3", "2o1", "0d01", "x1", "t3", "Pn", "0d02", "A002", "2o2", "2o3",
+    "2u12", "A402", "C1", "3u01", "0u03", "t1", "3u12", "C0", "t2", "Pt", "0u13", "0d03", "1d01", "2u11", "y3",
+    "y1", "+d1", "1u03", "y0", "y2", "Ps", "l1", "3o1", "1d02", "A424", "l3", "1d03", "A024", "0d11", "3o2", "1u13",
+    "2d02", "l0", "2d01", "3u11", "2u03", "l2", "Pl", "3o3", "0d12", "1d11", "A045", "2u13", "A445", "0d13", "1d12",
+    "3u13", "2d03", "M", "U0", "2d11", "U2", "1d13", "U1", "3u03", "3d01", "3d02", "2d12", "U3", "3d11", "3d03",
+    "2d13", "D1", "D0", "3d12", "D2", "3d13", "D3",
 )
 F32 = jnp.float32
 BF16 = jnp.bfloat16
@@ -60,7 +60,7 @@
     (
         out_ref, dx_ref, lora_ref,
         wqkv, wo, wup, wdn, small, lora_q, lora_v, vec_in, down_in,
-        xwin, uwin, qwin, kwin, vwin, dowin, stwin, mask,
+        xwin, uwin, qwin, kwin, vwin, dowin, stwin, mask, mixed,
         att, attf, stat, midb, norm1, stat1, hid, gelp, acc, gffn, gbuf, dq, dk_acc, dv_acc, dkv,
         lsend, lrecv1, lrecv2,
         lsem, ssem, rsem,
@@ -278,12 +278,12 @@
         fill(jnp.logical_and(dp == n_dp - 1, t >= 2), 4)
         fill(jnp.logical_and(dp == n_dp - 1, t == 3), 3)
 
-    def adapter(w):
-        uwin[w] = dot_nt(xwin[w], down_in[...]).astype(BF16)
+    def adapter(w, pos):
+        uwin[tile(pos)] = dot_nt(xwin[w], down_in[...]).astype(BF16)
 
     def proj(w, pos, s):
         y = dot(xwin[w], wqkv[s].reshape(width, 3 * 256))
-        u = uwin[w]
+        u = uwin[tile(pos), 0:LANES]
         place = (tile(pos), tile(s))
         q = y[:, :256] + dot(u, lora_q[s]) + small[s, 16:17, :]
         qwin[place] = (q * (1.0 / math.sqrt(HD))).astype(BF16)
@@ -292,7 +292,7 @@
         vwin[place] = v.astype(BF16)
 
     def proj_all(w, pos):
-        adapter(w)
+        adapter(w, pos)
 
         @pl.loop(0, 4)
         def _(s):
@@ -311,8 +311,9 @@
 
         def body(p, cols):
             q_heads = halves(qwin[tile(1), cols])
-            k, v = kwin[begin:end, cols], vwin[begin:end, cols]
-            before, outs, found = attf[:, cols], [], stat[...]
+            k = kwin[begin:end, cols]
+            v = jnp.concatenate([vwin[begin:end, cols], uwin[begin:end, LANES:]], axis=1)
+            before, outs, found, inputs = attf[:, cols], [], stat[...], mixed[...]
             for i in range(2):
                 s = dot_nt(q_heads[i], k) + mask[:, begin:end]
                 top = jnp.max(s, axis=1, keepdims=True)
@@ -322,20 +323,25 @@
                 e = jnp.exp(s - top)
                 total = jnp.sum(e, axis=1, keepdims=True)
                 o = dot(e.astype(BF16), v)
+                o, extra = o[:, :LANES], o[:, LANES:]
                 if lo:
                     alpha = jnp.exp(old - top)
                     total = total + column(16 + 2 * p + i) * alpha
                     o = o + before * alpha
+                    extra = extra + inputs * alpha
                 if hi == 5:
                     o = o * (1.0 / total)
+                    extra = extra * (1.0 / total)
                     top = top + jnp.log(total)
                 outs.append(o)
+                inputs = jnp.where(lane // 8 == 2 * p + i, extra, inputs)
                 found = jnp.where(lane == 2 * p + i, top, jnp.where(lane == 16 + 2 * p + i, total, found))
             o = jnp.where(first_half, outs[0], outs[1])
             attf[:, cols] = o
             if hi == 5:
                 att[:, cols] = o.astype(BF16)
             stat[...] = found
+            mixed[...] = inputs
 
         return body
 
@@ -421,67 +427,85 @@
             parts.append(dot(ds.astype(BF16), k))
         dq[:, cols] = (jnp.where(first_half, parts[0], parts[1]) * (1.0 / math.sqrt(HD))).astype(BF16)
 
-    def pass_keys(names, at, end, first=False, keys=True, values=True, unroll=1):
-        slots = [blocks[name][0] for name in names]
-        begin = blocks[names[0]][1] * rows
-        window = slice(begin, begin + len(names) * rows)
+    def pass_keys(pieces, at, end, first=False, unroll=1):
+        def joined(parts, axis):
+            return parts[0] if len(parts) == 1 else jnp.concatenate(parts, axis=axis)
+
+        windows = [slice(blocks[name][1] * rows + lo, blocks[name][1] * rows + hi) for name, lo, hi in pieces]
+        few = sum(hi - lo for _, lo, hi in pieces) <= 256
 
         def line(index):
-            parts = [stwin[w, pl.ds(index, 1), :] for w in slots]
-            return parts[0] if len(parts) == 1 else jnp.concatenate(parts, axis=1)
+            return joined([stwin[blocks[name][0], pl.ds(index, 1), :][:, lo:hi] for name, lo, hi in pieces], 1)
+
+        def products(heads, right):
+            if few:
+                both = dot_nt(jnp.concatenate(heads, axis=0), right)
+                return both[:256], both[256:]
+            return [dot_nt(head, right) for head in heads]
 
         def body(p, cols):
             k_heads, v_heads = halves(kwin[tile(1), cols]), halves(vwin[tile(1), cols])
-            q, do = qwin[window, cols], [dowin[w, :, cols] for w in slots]
-            do = do[0] if len(do) == 1 else jnp.concatenate(do, axis=0)
-            if len(slots) == 1:
-                scores = dot_nt(jnp.concatenate(k_heads, axis=0), q)
-                scores = [scores[:256], scores[256:]]
-                if keys:
-                    grads = dot_nt(jnp.concatenate(v_heads, axis=0), do)
-                    grads = [grads[:256], grads[256:]]
-            else:
-                scores = [dot_nt(k, q) for k in k_heads]
-                grads = [dot_nt(v, do) for v in v_heads]
+            q = joined([qwin[window, cols] for window in windows], 0)
+            do = joined([dowin[blocks[name][0], lo:hi, cols] for name, lo, hi in pieces], 0)
+            scores = products(k_heads, q)
+            grads = products(v_heads, do)
+            apart = joined([mask[:, window] for window in windows], 1)
             probs, ds = [], []
             for i in range(2):
-                prob = jnp.exp(scores[i] + mask[:, window] - line(2 * p + i))
-                if keys:
-                    ds.append((prob * (grads[i] - line(16 + 2 * p + i))).astype(BF16))
+                prob = jnp.exp(scores[i] + apart - line(2 * p + i))
+                ds.append((prob * (grads[i] - line(16 + 2 * p + i))).astype(BF16))
                 probs.append(prob.astype(BF16))
-            for total, lefts, right, wanted in ((dk_acc, ds, q, keys), (dv_acc, probs, do, values)):
-                if wanted:
-                    if len(slots) == 1:
-                        both = dot(jnp.concatenate(lefts, axis=0), right)
-                        both = jnp.where(first_half, both[:256], both[256:])
-                    else:
-                        both = jnp.where(first_half, dot(lefts[0], right), dot(lefts[1], right))
-                    total[:, cols] = both if first else total[:, cols] + both
+            for total, lefts, right in ((dk_acc, ds, q), (dv_acc, probs, do)):
+                if few:
+                    both = dot(jnp.concatenate(lefts, axis=0), right)
+                    both = jnp.where(first_half, both[:256], both[256:])
+                else:
+                    both = jnp.where(first_half, dot(lefts[0], right), dot(lefts[1], right))
+                total[:, cols] = both if first else total[:, cols] + both
 
         loop_pairs(at, end, body, unroll)
 
     def lora_partial():
-        u = uwin[2].astype(F32).T[0:16].astype(BF16)
-        is_query = lax.broadcasted_iota(jnp.int32, (16, 1), 0) < 8
+        u = uwin[tile(1), 0:LANES].astype(F32).T[0:16].astype(BF16)
+        of_queries = dot(u, dq[...])
+        each = dot(mixed[...].T.astype(BF16), dowin[2])
+        row_head = lax.broadcasted_iota(jnp.int32, each.shape, 0) // 8
+        column_head = lax.broadcasted_iota(jnp.int32, each.shape, 1) // HD
+        each = jnp.where(row_head == column_head, each, 0.0)
+        of_values = each[0:8]
+        for h in range(1, 16):
+            of_values = of_values + each[8 * h : 8 * h + 8]
+        both = jnp.concatenate([of_queries[0:8], of_values], axis=0)
         for s in range(4):
-            cols = slice(256 * s, 256 * s + 256)
-            both = jnp.where(is_query, dot(u, dq[:, cols]), dot(u, dkv[1, :, cols]))
-            lsend[s] = both
-
-    def input_gradient():
+            lsend[s] = both[:, 256 * s : 256 * s + 256]
+
+    def query_gradient():
         gu = jnp.zeros((rows, LANES), F32)
         for s in range(4):
-            cols = slice(256 * s, 256 * s + 256)
-            gu = gu + dot_nt(dq[:, cols], lora_q[s]) + dot_nt(dkv[1, :, cols], lora_v[s])
-        gu = gu.astype(BF16)
+            gu = gu + dot_nt(dq[:, 256 * s : 256 * s + 256], lora_q[s])
+        stat1[...] = gu
 
         @pl.loop(0, 4, unroll=4)
         def _(n):
-            total = acc[:, tile(n)] + dot(gu, down_in[:, tile(n)])
+            total = acc[:, tile(n)]
+            for s in range(4):
+                weight = wqkv[s, n, :, :, 0:256].reshape(256, 256)
+                total = total + dot_nt(dq[:, 256 * s : 256 * s + 256], weight)
+            acc[:, tile(n)] = total
+
+    def input_gradient():
+        gu = stat1[...]
+        for s in range(4):
+            gu = gu + dot_nt(dkv[1, :, 256 * s : 256 * s + 256], lora_v[s])
+        gu = gu.astype(BF16)
+
+        @pl.loop(0, 4, unroll=4)
+        def _(n):
+            total = acc[:, tile(n)] + dot(gu, down_in[0:LANES, tile(n)])
             for s in range(4):
                 cols = slice(256 * s, 256 * s + 256)
-                three = jnp.concatenate([dq[:, cols], dkv[0, :, cols], dkv[1, :, cols]], axis=1)
-                total = total + dot_nt(three, wqkv[s, n].reshape(256, 3 * 256))
+                two = jnp.concatenate([dkv[0, :, cols], dkv[1, :, cols]], axis=1)
+                total = total + dot_nt(two, wqkv[s, n, :, :, 256:].reshape(256, 512))
             att[:, tile(n)] = total.astype(BF16)
 
     def chunk(ref, first, size, loads):
@@ -491,7 +515,7 @@
     up0, up1 = chunk(wup, 0, 64, ld_up), chunk(wup, 64, 64, ld_up)
     dn0, dn1 = chunk(wdn, 0, 64, ld_dn), chunk(wdn, 64, 64, ld_dn)
     o0 = chunk(wo, 0, 32, ld_o)
-    quarter = rows // 4
+    half, quarter = rows // 2, rows // 4
     tok = [Exchange(xwin, i * quarter, quarter) for i in range(4)]
     small_base = alloc("recv", 4)
     wide = [Exchange(dowin, i * quarter, quarter) for i in range(4)]
@@ -515,7 +539,8 @@
         for j in range(4):
             small[t, 18 + j : 19 + j, cols] = ub_in[2 * j + i : 2 * j + i + 1, :].astype(F32)
     small[t, 22:24, :] = jnp.zeros((2, 256), F32)
-    maps = [qd_in[...].astype(F32), vd_in[...].astype(F32), jnp.zeros((LANES - 16, width), F32)]
+    value_map = vd_in[...].astype(F32)
+    maps = [qd_in[...].astype(F32), value_map, jnp.zeros((LANES - 16, width), F32)] + [value_map] * 16
     down_in[...] = jnp.concatenate(maps, axis=0).astype(BF16)
     pl.semaphore_wait(barrier, 3 + n_dp - 1)
     done(ld_x)
@@ -589,7 +614,7 @@
         elif item == "P20":
             setup()
             small_ready()
-            adapter(2)
+            adapter(2, 1)
             done(ld_qkv)
             proj(2, 1, t)
         elif item == "P2":
@@ -638,20 +663,20 @@
         elif kind == "Q":
             loop_pairs(int(rest), int(rest) + 2, pass_queries)
         elif kind == "K":
-            names, at = rest[:2], int(rest[2])
-            pass_keys(names, at, at + 4, first=names == "n2")
-        elif kind == "V":
-            pass_keys("l", 0, pairs, keys=False, unroll=2)
+            if rest[0] == "x":
+                lo = int(rest[1]) * half
+                pass_keys([("s", lo, lo + half), ("t", lo, lo + half)], 0, pairs, unroll=2)
+            elif rest[0] == "l":
+                pass_keys([("l", 0, rows)], 0, pairs, unroll=2)
+            else:
+                at = int(rest[2])
+                pass_keys([("n", 0, rows), ("2", 0, rows)], at, at + 4, first=True)
         elif kind == "G":
-            dkv[1] = dv_acc[...].astype(BF16)
             lora_partial()
             for d in range(1, 4):
                 peer = lax.rem(t + d, 4)
                 remote(lsend.at[peer], lrecv1.at[t], lora1 + t, (dp, peer))
             lrecv1[t] = lsend[t]
-        elif kind == "L":
-            pass_keys("l", 0, pairs, values=False, unroll=2)
-            dkv[0] = dk_acc[...].astype(BF16)
         elif kind == "H":
             for d in range(1, 4):
                 peer = lax.rem(t + d, 4)
@@ -659,7 +684,11 @@
             lrecv2[dp] = 2.0 * ((lrecv1[0] + lrecv1[1]) + (lrecv1[2] + lrecv1[3]))
             for d in range(1, n_dp):
                 remote(lrecv2.at[dp], lrecv2.at[dp], lora2 + dp, (lax.rem(dp + d, n_dp), t))
+        elif kind == "i":
+            query_gradient()
         elif kind == "I":
+            dkv[0] = dk_acc[...].astype(BF16)
+            dkv[1] = dv_acc[...].astype(BF16)
             input_gradient()
     dx_copy = local(att, dx_ref)
     for d in range(1, n_dp):
@@ -745,15 +774,16 @@
             vmem((4, 128, 256), BF16),
             vmem((4, 128, 256), BF16),
             vmem((8, width), F32),
-            vmem((LANES, width), BF16),
+            vmem((2 * LANES, width), BF16),
             vmem((6, rows, width), BF16),
-            vmem((5, rows, LANES), BF16),
+            vmem((window, 2 * LANES), BF16),
             vmem((window, width), BF16),
             vmem((window, width), BF16),
             vmem((window, width), BF16),
             vmem((6, rows, width), BF16),
             vmem((6, 32, rows), F32),
             vmem((rows, window), F32),
+            vmem((rows, LANES), F32),
             vmem(full, BF16),
             vmem(full, F32),
             vmem((rows, LANES), F32),

time: 178 us -> 166 us (0.933)
  Pallas kernels: 175 us -> 165 us
    pallas_call x1, Pallas kernels: 173 us -> 163 us  [shards(): call(tokens, cotangent, cut(query_proj_weight), cut(key_proj_weight), cut...]
where the time goes in v1:
time: 166 us
  Pallas kernels  165 us (99%)
    pallas_call x1, Pallas kernels, shards(): call(tokens, cotangent, cut(query_proj_weight), cut(key_proj_weight), cut...  163 us

profile of v1, /device:TPU:2, one launch (start us, length us, event | category | flops | bytes accessed | tf_op | source)
XLA Modules:
  0.0 165.7 jit_solution(7188914793053587887)
XLA Ops:
  0.6 162.8 %layer.1 = (bf16[256,1024]{1,0:T(8,128)(2,1)}, bf16[256,1024]{1,0:T(8,128)(2,1)}, f32[16,256]{1,0:T(8,128)}) custom-call(bf16[256,1024]{1,0:T(8,128)(2,1)} %refs_0_.1, bf16[256,1024]{1,0:T(8,128)(2,1)} %refs_1_.1, bf16[4,2,128,256]{3,2,1,0:T(8,128)(2,1)} %bitcast.20, bf16[4,2,128,256]{3,2,1,0:T(8,128)(2,1)} %bitcast.21, bf16[4,2,128,256]{3,2,1,0:T(8,128)(2,1)} %bitcast.22, ...), custom_call_target="tpu_custom_call" | custom-call | tf_op jit(solution)/shard_map/layer/pallas_call | solution.py:815
  163.5 2.0 %hand_over.1 = (bf16[256,1024]{1,0:T(8,128)(2,1)}, bf16[256,1024]{1,0:T(8,128)(2,1)}, f32[8,256]{1,0:T(8,128)}, f32[8,256]{1,0:T(8,128)}) custom-call(bf16[256,1024]{1,0:T(8,128)(2,1)} %get-tuple-element.7.out, bf16[256,1024]{1,0:T(8,128)(2,1)} %get-tuple-element.8.grad, f32[16,256]{1,0:T(8,128)} %get-tuple-element.9.lora), custom_call_target="tpu_custom_call" | custom-call | tf_op jit(solution)/shard_map/hand_over/pallas_call | solution.py:820

commit v2 on v1

--- a/solution.py
+++ b/solution.py
@@ -18,20 +18,20 @@
     "S": "first", "n": "neighbours", "c": "chain1", "C": "chain2", "x": "ends", "y": "chain3", "t": "third", "l": "last",
 }
 PLAN_BACK = (
-    "S1", "S0", "c1", "Q2", "n1", "S3", "c0", "Q0", "S2", "C1", "Q6", "n0", "n3", "Q4", "C0", "G", "x0", "n2", "c2",
-    "Kn20", "c3", "y0", "y1", "x1", "C2", "x3", "i", "Kn24", "t0", "t1", "C3", "l0", "x2", "y2", "Kx0", "H", "t2",
-    "l1", "t3", "l2", "y3", "Kx1", "l3", "Kl", "I", "J",
+    "S1", "T", "c1", "S0", "Q6", "S2", "n1", "c0", "Q4", "S3", "Q0", "x1", "C1", "c2", "n0", "Q2", "G", "c3", "x0",
+    "n2", "C0", "n3", "Kn20", "y1", "i", "x3", "t0", "C2", "y0", "H", "Kn24", "t3", "l1", "C3", "t1", "y2", "x2",
+    "Kx0", "l2", "y3", "t2", "Kx1", "l3", "l0", "J", "Kl", "I",
 )
 PLAN = (
-    "+q1", "+q0", "+u0", "S3", "0q11", "0q01", "1q11", "0u01", "1q01", "0q12", "0q02", "S2", "c3", "2q01", "1u01",
-    "1q12", "0u02", "S0", "2q11", "0q03", "0q13", "+o", "+u1", "S1", "n0", "1q03", "1q13", "1u02", "c2", "2q03",
-    "0o1", "1q02", "0u11", "2q12", "2u02", "0o2", "x0", "c1", "+d0", "2q13", "1o1", "P20", "0u12", "2q02", "0o3",
-    "n3", "3q11", "C3", "3q12", "3u02", "3q03", "n2", "3q13", "3q02", "1o2", "t0", "3q01", "n1", "x3", "P2", "C2",
-    "2u01", "1u12", "x2", "1u11", "c0", "1o3", "2o1", "0d01", "x1", "t3", "Pn", "0d02", "A002", "2o2", "2o3",
-    "2u12", "A402", "C1", "3u01", "0u03", "t1", "3u12", "C0", "t2", "Pt", "0u13", "0d03", "1d01", "2u11", "y3",
-    "y1", "+d1", "1u03", "y0", "y2", "Ps", "l1", "3o1", "1d02", "A424", "l3", "1d03", "A024", "0d11", "3o2", "1u13",
-    "2d02", "l0", "2d01", "3u11", "2u03", "l2", "Pl", "3o3", "0d12", "1d11", "A045", "2u13", "A445", "0d13", "1d12",
-    "3u13", "2d03", "M", "U0", "2d11", "U2", "1d13", "U1", "3u03", "3d01", "3d02", "2d12", "U3", "3d11", "3d03",
+    "+q1", "+q0", "+u0", "S3", "Z", "0q11", "0q01", "1q11", "0u01", "1q01", "0q12", "0q02", "S2", "c3", "2q01",
+    "1u01", "0u02", "1q12", "S0", "2q11", "0q03", "0q13", "+o", "+u1", "S1", "n0", "1q03", "1q13", "1u02", "c2",
+    "2q03", "0o1", "1q02", "0u11", "2q12", "2u02", "0o2", "x0", "c1", "+d0", "2q13", "1o1", "P0", "0u12", "2q02",
+    "0o3", "n3", "3q11", "C3", "3q12", "3u02", "3q03", "n2", "3q13", "2u01", "3q02", "1o2", "t0", "3q01", "n1",
+    "x3", "C2", "1u12", "x2", "1u11", "Pn", "c0", "1o3", "2o1", "0d01", "x1", "t3", "0d02", "A002", "2o2", "2o3",
+    "2u12", "A402", "C1", "3u01", "0u03", "t1", "3u12", "C0", "t2", "0u13", "0d03", "1d01", "2u11", "y3", "y1",
+    "+d1", "1u03", "y0", "y2", "Ps", "l1", "3o1", "1d02", "A424", "l3", "0d11", "1d03", "A024", "3o2", "1u13",
+    "2d02", "l0", "2d01", "3u11", "2u03", "l2", "Pl", "3o3", "0d12", "1d11", "A045", "2u13", "A445", "0d13", "M",
+    "1d12", "3u13", "2d03", "U0", "2d11", "U2", "1d13", "U1", "3u03", "3d01", "3d02", "2d12", "U3", "3d11", "3d03",
     "2d13", "D1", "D0", "3d12", "D2", "3d13", "D3",
 )
 F32 = jnp.float32
@@ -126,6 +126,11 @@
         )
         when(pred, copy.wait_recv)
 
+    def settle():
+        for pred, copy in pending.values():
+            when(pred, copy.wait_send)
+        pending.clear()
+
     def local(src, dst):
         copy = pltpu.make_async_copy(src, dst, lsem.at[alloc("local", 1)])
         copy.start()
@@ -146,8 +151,9 @@
             copies.pop().wait()
 
     class Chunk:
-        def __init__(self, ref, first, size, loads):
+        def __init__(self, ref, first, size, loads, by_y=None):
             self.ref, self.first, self.size, self.loads = ref, first, size, loads
+            self.by_y = by_y or size // 2
             self.zr = alloc("recv", 4)
             self.xr, self.yr, self.dr, self.cr = (alloc("recv", 3) - 1 for _ in range(4))
 
@@ -173,12 +179,12 @@
             remote(own, own, self.yr + a, y_dev)
 
         def stage1(self, a):
-            s, half = shard(a), self.size // 2
+            s = shard(a)
             arrived(self.region(s, yx_x), self.xr + a)
-            part = self.region(s, yx_x, 0, half)
+            part = self.region(s, yx_x, 0, self.by_y)
             remote(part, part, self.dr + a, y_dev)
             arrived(self.region(s, yx_y), self.yr + a)
-            part = self.region(s, yx_y, half, half)
+            part = self.region(s, yx_y, self.by_y, self.size - self.by_y)
             remote(part, part, self.dr + a, x_dev)
 
         def stage2(self, a):
@@ -278,25 +284,25 @@
         fill(jnp.logical_and(dp == n_dp - 1, t >= 2), 4)
         fill(jnp.logical_and(dp == n_dp - 1, t == 3), 3)
 
-    def adapter(w, pos):
-        uwin[tile(pos)] = dot_nt(xwin[w], down_in[...]).astype(BF16)
-
-    def proj(w, pos, s):
-        y = dot(xwin[w], wqkv[s].reshape(width, 3 * 256))
-        u = uwin[tile(pos), 0:LANES]
-        place = (tile(pos), tile(s))
-        q = y[:, :256] + dot(u, lora_q[s]) + small[s, 16:17, :]
-        qwin[place] = (q * (1.0 / math.sqrt(HD))).astype(BF16)
-        kwin[place] = y[:, 256:512].astype(BF16)
-        v = y[:, 512:] + dot(u, lora_v[s]) + small[s, 17:18, :]
-        vwin[place] = v.astype(BF16)
-
-    def proj_all(w, pos):
-        adapter(w, pos)
+    def project(names):
+        begin = blocks[names[0]][1] * rows
+        place = slice(begin, begin + len(names) * rows)
+
+        def tokens():
+            parts = [xwin[blocks[name][0]] for name in names]
+            return parts[0] if len(parts) == 1 else jnp.concatenate(parts, axis=0)
+
+        uwin[place] = dot_nt(tokens(), down_in[...]).astype(BF16)
 
         @pl.loop(0, 4)
         def _(s):
-            proj(w, pos, s)
+            y = dot(tokens(), wqkv[s].reshape(width, 3 * 256))
+            u = uwin[place, 0:LANES]
+            q = y[:, :256] + dot(u, lora_q[s]) + small[s, 16:17, :]
+            qwin[place, tile(s)] = (q * (1.0 / math.sqrt(HD))).astype(BF16)
+            kwin[place, tile(s)] = y[:, 256:512].astype(BF16)
+            v = y[:, 512:] + dot(u, lora_v[s]) + small[s, 17:18, :]
+            vwin[place, tile(s)] = v.astype(BF16)
 
     def loop_pairs(lo, hi, body, unroll=1):
         @pl.loop(lo, hi, unroll=unroll)
@@ -406,6 +412,7 @@
         def _(s):
             dowin[2, :, tile(s)] = dot_nt(gffn[...], wo[s].reshape(256, width)).astype(BF16)
 
+    def statistics():
         product = dowin[2].astype(F32) * attf[...]
         high = product.astype(BF16)
         low = (product - high.astype(F32)).astype(BF16)
@@ -498,18 +505,17 @@
         for s in range(4):
             gu = gu + dot_nt(dkv[1, :, 256 * s : 256 * s + 256], lora_v[s])
         gu = gu.astype(BF16)
-
-        @pl.loop(0, 4, unroll=4)
-        def _(n):
+        for n in range(4):
             total = acc[:, tile(n)] + dot(gu, down_in[0:LANES, tile(n)])
             for s in range(4):
                 cols = slice(256 * s, 256 * s + 256)
                 two = jnp.concatenate([dkv[0, :, cols], dkv[1, :, cols]], axis=1)
                 total = total + dot_nt(two, wqkv[s, n, :, :, 256:].reshape(256, 512))
             att[:, tile(n)] = total.astype(BF16)
-
-    def chunk(ref, first, size, loads):
-        return Chunk(ref, first, size, loads)
+            final.append(local(att.at[:, tile(n)], dx_ref.at[:, tile(n)]))
+
+    def chunk(*args):
+        return Chunk(*args)
 
     qkv0, qkv1 = chunk(wqkv, 0, 64, ld_qkv), chunk(wqkv, 64, 64, ld_qkv)
     up0, up1 = chunk(wup, 0, 64, ld_up), chunk(wup, 64, 64, ld_up)
@@ -523,30 +529,31 @@
     lora1 = alloc("recv", 4)
     lora2 = alloc("recv", n_dp)
 
-    clear(xwin)
-    done(ld_small)
-    for i in range(8):
-        cols = slice(LANES * i, LANES * i + LANES)
-        for j, ref in enumerate(vec_refs):
-            vec_in[j : j + 1, cols] = ref[i : i + 1, :].astype(F32)
-    own_small = [2.0 * qu_in[...].astype(F32), 2.0 * vu_in[...].astype(F32)]
-    small[t, 0:8, :] = own_small[0]
-    small[t, 8:16, :] = own_small[1]
-    for i in range(2):
-        cols = slice(LANES * i, LANES * i + LANES)
-        small[t, 16:17, cols] = qb_in[i : i + 1, :].astype(F32)
-        small[t, 17:18, cols] = vb_in[i : i + 1, :].astype(F32)
-        for j in range(4):
-            small[t, 18 + j : 19 + j, cols] = ub_in[2 * j + i : 2 * j + i + 1, :].astype(F32)
-    small[t, 22:24, :] = jnp.zeros((2, 256), F32)
-    value_map = vd_in[...].astype(F32)
-    maps = [qd_in[...].astype(F32), value_map, jnp.zeros((LANES - 16, width), F32)] + [value_map] * 16
-    down_in[...] = jnp.concatenate(maps, axis=0).astype(BF16)
+    def prepare():
+        for ref in (xwin, dowin, stwin):
+            clear(ref)
+        done(ld_small)
+        for i in range(8):
+            cols = slice(LANES * i, LANES * i + LANES)
+            for j, ref in enumerate(vec_refs):
+                vec_in[j : j + 1, cols] = ref[i : i + 1, :].astype(F32)
+        own_small = [2.0 * qu_in[...].astype(F32), 2.0 * vu_in[...].astype(F32)]
+        small[t, 0:8, :] = own_small[0]
+        small[t, 8:16, :] = own_small[1]
+        for i in range(2):
+            cols = slice(LANES * i, LANES * i + LANES)
+            small[t, 16:17, cols] = qb_in[i : i + 1, :].astype(F32)
+            small[t, 17:18, cols] = vb_in[i : i + 1, :].astype(F32)
+            for j in range(4):
+                small[t, 18 + j : 19 + j, cols] = ub_in[2 * j + i : 2 * j + i + 1, :].astype(F32)
+        small[t, 22:24, :] = jnp.zeros((2, 256), F32)
+        value_map = vd_in[...].astype(F32)
+        maps = [qd_in[...].astype(F32), value_map, jnp.zeros((LANES - 16, width), F32)] + [value_map] * 16
+        down_in[...] = jnp.concatenate(maps, axis=0).astype(BF16)
+        for d in range(1, 4):
+            remote(small.at[t], small.at[t], small_base + t, (dp, lax.rem(t + d, 4)))
+
     pl.semaphore_wait(barrier, 3 + n_dp - 1)
-    done(ld_x)
-    for d in range(1, 4):
-        remote(small.at[t], small.at[t], small_base + t, (dp, lax.rem(t + d, 4)))
-
     near = jnp.where(t < 3, 3, 1)
     second = jnp.where(lax.rem(t, 2) == 0, 4, 0)
     third = jnp.where(t == 0, 0, jnp.where(t == 3, 4, 1))
@@ -610,21 +617,16 @@
         elif kind in "0123":
             getattr(named[rest[:-1]], "stage" + kind)(int(rest[-1]))
         elif kind in STEPS:
+            done(ld_x)
             getattr(tok[int(rest)], STEPS[kind])()
-        elif item == "P20":
+        elif kind == "Z":
+            prepare()
+        elif item == "P0":
             setup()
             small_ready()
-            adapter(2, 1)
+        elif kind == "P":
             done(ld_qkv)
-            proj(2, 1, t)
-        elif item == "P2":
-
-            @pl.loop(1, 4)
-            def _(a):
-                proj(2, 1, shard(a))
-
-        elif kind == "P":
-            proj_all(*blocks[rest])
+            project({"n": "n2", "s": "st", "l": "l"}[rest])
         elif kind == "A":
             at, lo, hi = (int(i) for i in rest)
             loop_pairs(at, at + 4, attend(lo, hi))
@@ -642,9 +644,7 @@
 
     done(ld_cot)
     second_norm()
-    out_copy = local(midb, out_ref)
-    clear(dowin)
-    clear(stwin)
+    final = [local(midb, out_ref)]
 
     @pl.loop(0, 4)
     def _(s):
@@ -658,8 +658,12 @@
 
     for item in PLAN_BACK:
         kind, rest = item[0], item[1:]
+        if item == "l3":
+            settle()
         if kind in STEPS:
             swap(STEPS[kind], int(rest))
+        elif kind == "T":
+            statistics()
         elif kind == "Q":
             loop_pairs(int(rest), int(rest) + 2, pass_queries)
         elif kind == "K":
@@ -684,36 +688,35 @@
             lrecv2[dp] = 2.0 * ((lrecv1[0] + lrecv1[1]) + (lrecv1[2] + lrecv1[3]))
             for d in range(1, n_dp):
                 remote(lrecv2.at[dp], lrecv2.at[dp], lora2 + dp, (lax.rem(dp + d, n_dp), t))
+        elif kind == "J":
+            for d in range(1, n_dp):
+                peer = lax.rem(dp + d, n_dp)
+                arrived(lrecv2.at[peer], lora2 + peer)
+            total = lrecv2[0]
+            for i in range(1, n_dp):
+                total = total + lrecv2[i]
+            lsend[0] = total
+            final.append(local(lsend.at[0], lora_ref))
         elif kind == "i":
             query_gradient()
         elif kind == "I":
             dkv[0] = dk_acc[...].astype(BF16)
             dkv[1] = dv_acc[...].astype(BF16)
             input_gradient()
-    dx_copy = local(att, dx_ref)
-    for d in range(1, n_dp):
-        peer = lax.rem(dp + d, n_dp)
-        arrived(lrecv2.at[peer], lora2 + peer)
-    total = lrecv2[0]
-    for i in range(1, n_dp):
-        total = total + lrecv2[i]
-    lora_ref[...] = total
-    dx_copy.wait()
-    out_copy.wait()
-    for pred, copy in pending.values():
-        when(pred, copy.wait_send)
+    settle()
+    done(final)
     assert count["recv"] <= rsem.shape[0] and count["local"] <= lsem.shape[0]
 
 
 def hand_over(out, grad, lora, out_to, grad_to, query_to, value_to, out_at, grad_at, lora_at, sems):
-    rows = out.shape[0] // 2
-    halves = [pl.ds(i * rows, rows) for i in range(2)]
+    rows = out.shape[0] // 4
+    parts = [pl.ds(i * rows, rows) for i in range(4)]
     loads = [(lora, lora_at)]
     stores = [[(lora_at.at[0:8], query_to), (lora_at.at[8:16], value_to)]]
     for source, at, to in ((out, out_at, out_to), (grad, grad_at, grad_to)):
-        for half in halves:
-            loads.append((source.at[half], at.at[half]))
-            stores.append([(at.at[half], to.at[half])])
+        for part in parts:
+            loads.append((source.at[part], at.at[part]))
+            stores.append([(at.at[part], to.at[part])])
     copies = [pltpu.make_async_copy(a, b, sems.at[i]) for i, (a, b) in enumerate(loads)]
     for copy in copies:
         copy.start()
@@ -764,7 +767,7 @@
             jax.ShapeDtypeStruct((16, 256), F32),
         ),
         in_specs=[any_spec] * 22,
-        out_specs=(any_spec, any_spec, vmem_spec),
+        out_specs=(any_spec,) * 3,
         scratch_shapes=[
             vmem((4, 4, 2, 128, 768), BF16),
             vmem((4, 4, 2, 32, 1024), BF16),
@@ -802,7 +805,7 @@
             vmem((4, 16, 256), F32),
             vmem((4, 16, 256), F32),
             vmem((n_dp, 16, 256), F32),
-            pltpu.SemaphoreType.DMA((26,)),
+            pltpu.SemaphoreType.DMA((30,)),
             pltpu.SemaphoreType.DMA((48,)),
             pltpu.SemaphoreType.DMA((174 + n_dp,)),
         ]
@@ -823,7 +826,7 @@
         in_specs=[any_spec] * 3,
         out_specs=(any_spec,) * 4,
         scratch_shapes=[
-            vmem(full, BF16), vmem(full, BF16), vmem((2 * rank, 256), F32), pltpu.SemaphoreType.DMA((11,))
+            vmem(full, BF16), vmem(full, BF16), vmem((2 * rank, 256), F32), pltpu.SemaphoreType.DMA((19,))
         ],
         name="hand_over",
     )(out, grad, lora)

time: 166 us -> 164 us (0.988)
  Pallas kernels: 165 us -> 162 us
    pallas_call x1, Pallas kernels: 163 us -> 160 us  [shards(): call(tokens, cotangent, cut(query_proj_weight), cut(key_proj_weight), cut...]
where the time goes in v2:
time: 164 us; the launch traced here: 163 us
  Pallas kernels  162 us (99%)
    pallas_call x1, Pallas kernels, shards(): call(tokens, cotangent, cut(query_proj_weight), cut(key_proj_weight), cut...  160 us

profile of v2, /device:TPU:2, one launch (start us, length us, event | category | flops | bytes accessed | tf_op | source)
XLA Modules:
  0.0 163.3 jit_solution(2006399160486613014)
XLA Ops:
  0.6 160.3 %layer.1 = (bf16[256,1024]{1,0:T(8,128)(2,1)}, bf16[256,1024]{1,0:T(8,128)(2,1)}, f32[16,256]{1,0:T(8,128)}) custom-call(bf16[256,1024]{1,0:T(8,128)(2,1)} %refs_0_.1, bf16[256,1024]{1,0:T(8,128)(2,1)} %refs_1_.1, bf16[4,2,128,256]{3,2,1,0:T(8,128)(2,1)} %bitcast.20, bf16[4,2,128,256]{3,2,1,0:T(8,128)(2,1)} %bitcast.21, bf16[4,2,128,256]{3,2,1,0:T(8,128)(2,1)} %bitcast.22, ...), custom_call_target="tpu_custom_call" | custom-call | tf_op jit(solution)/shard_map/layer/pallas_call | solution.py:818
  161.0 2.1 %hand_over.1 = (bf16[256,1024]{1,0:T(8,128)(2,1)}, bf16[256,1024]{1,0:T(8,128)(2,1)}, f32[8,256]{1,0:T(8,128)}, f32[8,256]{1,0:T(8,128)}) custom-call(bf16[256,1024]{1,0:T(8,128)(2,1)} %get-tuple-element.7.out, bf16[256,1024]{1,0:T(8,128)(2,1)} %get-tuple-element.8.grad, f32[16,256]{1,0:T(8,128)} %get-tuple-element.9.lora), custom_call_target="tpu_custom_call" | custom-call | tf_op jit(solution)/shard_map/hand_over/pallas_call | solution.py:823

commit v3 on v2

--- a/solution.py
+++ b/solution.py
@@ -55,8 +55,7 @@
     x_in, cot_in, wq_in, wk_in, wv_in, wo_in, wup_in, wdn_in,
     len_in, qd_in, vd_in, qu_in, vu_in, qb_in, vb_in, ub_in, *rest
 ):
-    small_from = (len_in, qd_in, vd_in, qu_in, vu_in, qb_in, vb_in, ub_in, *rest[:6])
-    rest = rest[6:]
+    vec_refs, rest = rest[:6], rest[6:]
     (
         out_ref, dx_ref, lora_ref,
         wqkv, wo, wup, wdn, small, lora_q, lora_v, vec_in, down_in,
@@ -64,9 +63,7 @@
         att, attf, stat, midb, norm1, stat1, hid, gelp, acc, gffn, gbuf, dq, dk_acc, dv_acc, dkv,
         lsend, lrecv1, lrecv2,
         lsem, ssem, rsem,
-        *small_to,
     ) = rest
-    len_in, qd_in, vd_in, qu_in, vu_in, qb_in, vb_in, ub_in, *vec_refs = small_to
     rows = x_in.shape[0]
     width = x_in.shape[1]
     pairs = width // LANES
@@ -136,7 +133,6 @@
         copy.start()
         return copy
 
-    ld_small = [local(a, b) for a, b in zip(small_from, small_to)]
     ld_qkv = [
         local(w, wqkv.at[t, :, :, :, pl.ds(256 * i, 256)]) for i, w in enumerate((wq_in, wk_in, wv_in))
     ]
@@ -532,7 +528,6 @@
     def prepare():
         for ref in (xwin, dowin, stwin):
             clear(ref)
-        done(ld_small)
         for i in range(8):
             cols = slice(LANES * i, LANES * i + LANES)
             for j, ref in enumerate(vec_refs):
@@ -629,7 +624,7 @@
             project({"n": "n2", "s": "st", "l": "l"}[rest])
         elif kind == "A":
             at, lo, hi = (int(i) for i in rest)
-            loop_pairs(at, at + 4, attend(lo, hi))
+            loop_pairs(at, at + 4, attend(lo, hi), 2)
         elif kind == "M":
             done(ld_o)
             after_attention()
@@ -766,7 +761,7 @@
             jax.ShapeDtypeStruct(full, BF16),
             jax.ShapeDtypeStruct((16, 256), F32),
         ),
-        in_specs=[any_spec] * 22,
+        in_specs=[any_spec] * 8 + [vmem_spec] * 14,
         out_specs=(any_spec,) * 3,
         scratch_shapes=[
             vmem((4, 4, 2, 128, 768), BF16),
@@ -805,11 +800,10 @@
             vmem((4, 16, 256), F32),
             vmem((4, 16, 256), F32),
             vmem((n_dp, 16, 256), F32),
-            pltpu.SemaphoreType.DMA((30,)),
+            pltpu.SemaphoreType.DMA((16,)),
             pltpu.SemaphoreType.DMA((48,)),
             pltpu.SemaphoreType.DMA((174 + n_dp,)),
-        ]
-        + [vmem(a.shape, a.dtype) for a in small_arrays],
+        ],
         compiler_params=pltpu.CompilerParams(
             collective_id=0, has_side_effects=True, vmem_limit_bytes=63 * 2**20
         ),

time: 164 us -> 164 us (level)
  no operation moved by 1% of the time
where the time goes in v3:
time: 164 us; the launch traced here: 163 us
  Pallas kernels  163 us (99%)
    pallas_call x1, Pallas kernels, shards(): call(tokens, cotangent, cut(query_proj_weight), cut(key_proj_weight), cut...  160 us

profile of v3, /device:TPU:2, one launch (start us, length us, event | category | flops | bytes accessed | tf_op | source)
XLA Modules:
  0.0 163.3 jit_solution(9723704391285689834)
XLA Ops:
  0.6 160.4 %layer.1 = (bf16[256,1024]{1,0:T(8,128)(2,1)}, bf16[256,1024]{1,0:T(8,128)(2,1)}, f32[16,256]{1,0:T(8,128)}) custom-call(bf16[256,1024]{1,0:T(8,128)(2,1)} %refs_0_.1, bf16[256,1024]{1,0:T(8,128)(2,1)} %refs_1_.1, bf16[4,2,128,256]{3,2,1,0:T(8,128)(2,1)} %bitcast.20, bf16[4,2,128,256]{3,2,1,0:T(8,128)(2,1)} %bitcast.21, bf16[4,2,128,256]{3,2,1,0:T(8,128)(2,1)} %bitcast.22, ...), custom_call_target="tpu_custom_call" | custom-call | tf_op jit(solution)/shard_map/layer/pallas_call | solution.py:812
  161.0 2.1 %hand_over.1 = (bf16[256,1024]{1,0:T(8,128)(2,1)}, bf16[256,1024]{1,0:T(8,128)(2,1)}, f32[8,256]{1,0:T(8,128)}, f32[8,256]{1,0:T(8,128)}) custom-call(bf16[256,1024]{1,0:T(8,128)(2,1)} %get-tuple-element.7.out, bf16[256,1024]{1,0:T(8,128)(2,1)} %get-tuple-element.8.grad, f32[16,256]{1,0:T(8,128)} %get-tuple-element.9.lora), custom_call_target="tpu_custom_call" | custom-call | tf_op jit(solution)/shard_map/hand_over/pallas_call | solution.py:817

commit v4 on v3

--- a/solution.py
+++ b/solution.py
@@ -290,7 +290,7 @@
 
         uwin[place] = dot_nt(tokens(), down_in[...]).astype(BF16)
 
-        @pl.loop(0, 4)
+        @pl.loop(0, 4, unroll=2 if len(names) == 1 else 1)
         def _(s):
             y = dot(tokens(), wqkv[s].reshape(width, 3 * 256))
             u = uwin[place, 0:LANES]
@@ -801,7 +801,7 @@
             vmem((4, 16, 256), F32),
             vmem((n_dp, 16, 256), F32),
             pltpu.SemaphoreType.DMA((16,)),
-            pltpu.SemaphoreType.DMA((48,)),
+            pltpu.SemaphoreType.DMA((32,)),
             pltpu.SemaphoreType.DMA((174 + n_dp,)),
         ],
         compiler_params=pltpu.CompilerParams(

time: 164 us -> 163 us (level)
  no operation moved by 1% of the time
where the time goes in v4:
time: 163 us
  Pallas kernels  162 us (99%)
    pallas_call x1, Pallas kernels, shards(): call(tokens, cotangent, cut(query_proj_weight), cut(key_proj_weight), cut...  160 us

profile of v4, /device:TPU:2, one launch (start us, length us, event | category | flops | bytes accessed | tf_op | source)
XLA Modules:
  0.0 162.8 jit_solution(4080552146144508592)
XLA Ops:
  0.6 159.9 %layer.1 = (bf16[256,1024]{1,0:T(8,128)(2,1)}, bf16[256,1024]{1,0:T(8,128)(2,1)}, f32[16,256]{1,0:T(8,128)}) custom-call(bf16[256,1024]{1,0:T(8,128)(2,1)} %refs_0_.1, bf16[256,1024]{1,0:T(8,128)(2,1)} %refs_1_.1, bf16[4,2,128,256]{3,2,1,0:T(8,128)(2,1)} %bitcast.20, bf16[4,2,128,256]{3,2,1,0:T(8,128)(2,1)} %bitcast.21, bf16[4,2,128,256]{3,2,1,0:T(8,128)(2,1)} %bitcast.22, ...), custom_call_target="tpu_custom_call" | custom-call | tf_op jit(solution)/shard_map/layer/pallas_call | solution.py:812
  160.5 2.1 %hand_over.1 = (bf16[256,1024]{1,0:T(8,128)(2,1)}, bf16[256,1024]{1,0:T(8,128)(2,1)}, f32[8,256]{1,0:T(8,128)}, f32[8,256]{1,0:T(8,128)}) custom-call(bf16[256,1024]{1,0:T(8,128)(2,1)} %get-tuple-element.7.out, bf16[256,1024]{1,0:T(8,128)(2,1)} %get-tuple-element.8.grad, f32[16,256]{1,0:T(8,128)} %get-tuple-element.9.lora), custom_call_target="tpu_custom_call" | custom-call | tf_op jit(solution)/shard_map/hand_over/pallas_call | solution.py:817
